TPU v7x, 32 devices: a whole 2x2x4 slice. The times are simulated.
32 devices in a mesh: dp: 8 (over z, x), seq: 4 (over y, core).
Axes of the slice: x: 2, y: 2, z: 4, core: 2. Of those that a mesh axis runs over, the one named last changes fastest.
Arguments:
- tokens: bfloat16 [8, 2048, 2048], P('dp', 'seq'), may hold values from -60 to 60
- in_gain: float32 [2048], replicated, may hold values from 0.1 to 1.9
- in_weight: bfloat16 [2048, 2304], P('dp'), may hold values from -0.125 to 0.125
- conv_weight: float32 [4, 2304], replicated, may hold values from -5 to 5
- conv_bias: float32 [2304], replicated, may hold values from -3 to 3
- log_decay: float32 [8, 32, 2048], P('dp', None, 'seq'), may hold values from -0.9 to 0
- skip: float32 [32], replicated, may hold values from 0.05 to 1
- out_gain: float32 [2048], replicated, may hold values from 0.1 to 1.9
- scan_order: int32 [512], replicated, may hold values from 0 to 511, each once
Outputs:
- regrouped: bfloat16 [8, 2048, 2048], P('dp', 'seq')
Inputs may be any that keep to these rules, and one draw needn't show every extreme that they name: Each of the 512 positions appears once; the q-th position of a frame in the next layer's scan is scan_order[q].
All inputs are finite; a program needn't handle non-finite values.
Results may differ from a plain program's by a relative error of at most 0.008.
Values may be sent and summed in bfloat16 or wider, within the bound.
A program may use at most 128 MiB of HBM per device.

v0:
```python
import functools
import math

import jax
import jax.numpy as jnp
from jax import lax
from jax.experimental import pallas as pl
from jax.experimental.pallas import tpu as pltpu
from jax.sharding import PartitionSpec as P

GROUP = 128
CHUNK = 256
HALO = 16
WINDOW = 3
LAG = 2
BF16 = jnp.bfloat16
F32 = jnp.float32
MESH = pl.DeviceIdType.MESH


def fused_kernel(
    sizes,
    tokens_hbm,
    gain_hbm,
    weight_hbm,
    conv_weight_hbm,
    conv_bias_hbm,
    decay_hbm,
    skip_hbm,
    out_gain_hbm,
    order_hbm,
    result_ref,
    tokens_ref,
    gain_ref,
    conv_weight_ref,
    conv_bias_ref,
    decay_ref,
    skip_ref,
    out_gain_ref,
    order_ref,
    skip_held,
    bias_held,
    arrived,
    together,
    slabs,
    normed,
    choice,
    down_held,
    down_decay_held,
    across_held,
    decay_held,
    projected,
    mixed,
    b_turned,
    c_held,
    scores,
    block_states,
    entering_half,
    intra,
    expanded,
    arriving_state,
    leaving_state,
    normalized,
    picked,
    z_send,
    z_recv,
    x_send,
    x_recv,
    core_send,
    core_recv,
    halo_send,
    halo_recv,
    state_send,
    state_recv,
    out_send,
    out_recv,
    own_sem,
    token_sem,
    weight_sem,
    small_sem,
):
    z_count, x_count, core_count, seq_count, head_width = sizes
    head_count = CHUNK // head_width
    dp = lax.axis_index("dp")
    seq = lax.axis_index("seq")
    z = dp // x_count
    x = dp % x_count
    core = seq % core_count
    sibling = seq - core + (core + 1) % core_count
    half = slabs.shape[4]
    slab_count = slabs.shape[0]
    chunk_count = slab_count - 1
    token_count, width = tokens_ref.shape
    block_count = token_count // GROUP
    positions = order_ref.shape[1]
    share = positions // seq_count

    partners = [(((z + k) % z_count) * x_count + x, seq) for k in range(1, z_count)]
    partners += [(z * x_count + (x + k) % x_count, seq) for k in range(1, x_count)]
    partners += [(dp, (seq + k) % seq_count) for k in range(1, seq_count)]
    barrier = pltpu.get_barrier_semaphore()
    for partner in partners:
        pl.semaphore_signal(barrier, inc=1, device_id=partner, device_id_type=MESH)

    own_rows = pl.ds(pl.multiple_of(core * half, half), half)

    def load_weight(slab):
        first = chunk_count * CHUNK if slab == 0 else (slab - 1) * CHUNK
        return pltpu.make_async_copy(
            weight_hbm.at[own_rows, first : first + CHUNK],
            slabs.at[slab, z, x, core],
            weight_sem.at[slab],
        )

    def load_tokens(block):
        rows = slice(block * GROUP, (block + 1) * GROUP)
        return pltpu.make_async_copy(tokens_hbm.at[rows], tokens_ref.at[rows], token_sem.at[block])

    small = [
        pltpu.make_async_copy(source, target, small_sem.at[i])
        for i, (source, target) in enumerate(
            [
                (gain_hbm, gain_ref),
                (conv_weight_hbm, conv_weight_ref),
                (conv_bias_hbm, conv_bias_ref),
                (decay_hbm, decay_ref),
                (skip_hbm, skip_ref),
                (out_gain_hbm, out_gain_ref),
                (order_hbm, order_ref),
            ]
        )
    ]
    for slab in range(slab_count):
        load_weight(slab).start()
    for block in range(block_count):
        load_tokens(block).start()
    for copy in small:
        copy.start()
    for slab in range(slab_count):
        load_weight(slab).wait()
    pl.semaphore_wait(barrier, len(partners))

    def z_copy(slab, k, source):
        return pltpu.make_async_remote_copy(
            src_ref=slabs.at[slab, source, x, core],
            dst_ref=slabs.at[slab, source, x, core],
            send_sem=z_send.at[slab, k - 1],
            recv_sem=z_recv.at[slab, k - 1],
            device_id=(((z + k) % z_count) * x_count + x, seq),
            device_id_type=MESH,
        )

    def x_copy(slab, k, source, row):
        piece = slabs.at[slab, row, source, core]
        return pltpu.make_async_remote_copy(
            src_ref=piece,
            dst_ref=piece,
            send_sem=x_send.at[slab, k - 1],
            recv_sem=x_recv.at[slab, k - 1],
            device_id=(z * x_count + (x + k) % x_count, seq),
            device_id_type=MESH,
        )

    def core_copy(slab, source):
        return pltpu.make_async_remote_copy(
            src_ref=slabs.at[slab, :, :, source],
            dst_ref=slabs.at[slab, :, :, source],
            send_sem=core_send.at[slab],
            recv_sem=core_recv.at[slab],
            device_id=(dp, sibling),
            device_id_type=MESH,
        )

    def send_own(slab):
        for k in range(1, z_count):
            z_copy(slab, k, z).start()
        for k in range(1, x_count):
            x_copy(slab, k, x, z).start()

    def pass_x(slab):
        for k in range(1, z_count):
            row = (z + z_count - k) % z_count
            z_copy(slab, k, row).wait_recv()
            for kx in range(1, x_count):
                x_copy(slab, kx, x, row).start()

        if isinstance(slab, int):
            if slab + WINDOW < slab_count:
                send_own(slab + WINDOW)
        else:

            @pl.when(slab + WINDOW < slab_count)
            def _():
                send_own(slab + WINDOW)

    def pass_core(slab):
        for k in range(1, x_count):
            x_copy(slab, k, (x + x_count - k) % x_count, slice(None)).wait_recv()
        if core_count > 1:
            core_copy(slab, core).start()

    def whole_slab(slab):
        if core_count > 1:
            core_copy(slab, (core + 1) % core_count).wait_recv()

    for slab in range(min(WINDOW, slab_count)):
        send_own(slab)

    for copy in small:
        copy.wait()
    for block in range(block_count):
        load_tokens(block).wait()
        rows = tokens_ref[block * GROUP : (block + 1) * GROUP, :].astype(F32)
        inverse = lax.rsqrt(jnp.mean(rows * rows, axis=1, keepdims=True) + 1e-05)
        normed[HALO + block * GROUP : HALO + (block + 1) * GROUP, :] = (
            rows * inverse * gain_ref[...]
        ).astype(BF16)

    halo_copy = pltpu.make_async_remote_copy(
        src_ref=normed.at[token_count : token_count + HALO],
        dst_ref=normed.at[0:HALO],
        send_sem=halo_send,
        recv_sem=halo_recv,
        device_id=(dp, (seq + 1) % seq_count),
        device_id_type=MESH,
    )

    @pl.when(seq < seq_count - 1)
    def _():
        halo_copy.start()

    @pl.when(seq == 0)
    def _():
        normed[0:HALO, :] = jnp.zeros((HALO, width), BF16)

    row_at = lax.broadcasted_iota(jnp.int32, (GROUP, GROUP), 0)
    column_at = lax.broadcasted_iota(jnp.int32, (GROUP, GROUP), 1)
    causal = column_at <= row_at
    lower = jnp.where(causal, 1.0, 0.0).astype(F32)
    unit = jnp.where(row_at == column_at, 1.0, 0.0).astype(F32)
    upper = jnp.where(row_at <= column_at, 1.0, 0.0).astype(F32)
    first_head = lax.broadcasted_iota(jnp.int32, (1, GROUP), 1) < head_width
    same_head = jnp.where(row_at // head_width == column_at // head_width, 1.0, 0.0).astype(BF16)
    same_head_twice = jnp.concatenate([same_head, same_head], axis=0)

    def project(slab, first_column):
        columns = pl.ds(first_column, CHUNK)
        matrix = slabs[slab].reshape(width, CHUNK)
        projected[...] = (
            jnp.dot(normed[...], matrix, preferred_element_type=F32).astype(BF16).astype(F32)
        )
        taps = conv_weight_ref.shape[0]
        for block in range(block_count):
            total = bias_held[slab]
            for tap in range(taps):
                first = HALO + block * GROUP + tap - (taps - 1)
                total = total + conv_weight_ref[tap : tap + 1, columns] * projected[
                    first : first + GROUP, :
                ]
            mixed[block * GROUP : (block + 1) * GROUP, :] = (
                0.5 * total * (1.0 + jnp.tanh(0.5 * total))
            ).astype(BF16)

    def both(columns, pair):
        return jnp.where(
            first_head, columns[:, 2 * pair : 2 * pair + 1], columns[:, 2 * pair + 1 : 2 * pair + 2]
        )

    pass_x(0)
    for slab in range(slab_count):
        first = chunk_count * CHUNK if slab == 0 else (slab - 1) * CHUNK
        bias_held[slab] = conv_bias_ref[first : first + CHUNK].reshape(1, CHUNK)
    for chunk in range(chunk_count):
        for pair in range(head_count // 2):
            head = chunk * head_count + 2 * pair
            skip_held[chunk, :, pair * GROUP : (pair + 1) * GROUP] = jnp.where(
                first_head, skip_ref[:, head : head + 1], skip_ref[:, head + 1 : head + 2]
            )
    for block in range(block_count):
        rows = slice(block * GROUP, (block + 1) * GROUP)
        decay = decay_ref[:, rows]
        across = jnp.dot(decay, upper, precision=lax.Precision.HIGHEST, preferred_element_type=F32)
        turned = (((1,), (1,)), ((), ()))
        down = lax.dot_general(
            lower, decay, turned, precision=lax.Precision.HIGHEST, preferred_element_type=F32
        )
        down_decay = lax.dot_general(
            unit, decay, turned, precision=lax.Precision.HIGHEST, preferred_element_type=F32
        )
        for chunk in range(chunk_count):
            heads = slice(chunk * head_count, (chunk + 1) * head_count)
            down_held[chunk, rows, :head_count] = down[:, heads]
            down_decay_held[chunk, rows, :head_count] = down_decay[:, heads]
            across_held[chunk, :head_count, rows] = across[heads, :]
            decay_held[chunk, :head_count, rows] = decay[heads, :]
    pass_core(0)
    pass_x(1)
    choice[...] = jnp.transpose(
        jnp.where(
            lax.broadcasted_iota(jnp.int32, (positions, positions), 0) == order_ref[...], 1.0, 0.0
        ).astype(F32)
    ).astype(BF16)

    @pl.when(seq > 0)
    def _():
        halo_copy.wait_recv()

    whole_slab(0)
    project(0, chunk_count * CHUNK)
    pass_x(2)
    pass_core(1)
    for block in range(block_count):
        rows = slice(block * GROUP, (block + 1) * GROUP)
        b_block = mixed[rows, :GROUP]
        c_block = mixed[rows, GROUP:]
        c_held[block] = c_block
        b_turned[block] = jnp.transpose(b_block.astype(F32)).astype(BF16)
        scores[block] = jnp.where(
            causal, jnp.dot(c_block, b_turned[block], preferred_element_type=F32), 0.0
        )
    def state_copy(chunk):
        return pltpu.make_async_remote_copy(
            src_ref=leaving_state.at[chunk],
            dst_ref=arriving_state.at[chunk],
            send_sem=state_send.at[chunk],
            recv_sem=state_recv.at[chunk],
            device_id=(dp, (seq + 1) % seq_count),
            device_id_type=MESH,
        )

    def out_columns(chunk):
        return pl.ds(pl.multiple_of(chunk * CHUNK, CHUNK), CHUNK)

    def out_copy(chunk, k, source):
        target = (seq + k) % seq_count
        return pltpu.make_async_remote_copy(
            src_ref=picked.at[chunk, pl.ds(pl.multiple_of(target * share, share), share)],
            dst_ref=arrived.at[chunk, source],
            send_sem=out_send.at[chunk, k - 1],
            recv_sem=out_recv.at[chunk, k - 1],
            device_id=(dp, target),
            device_id_type=MESH,
        )

    step = min(share, max(GROUP // seq_count, 16))
    mixed_rows = step * seq_count
    row = lax.broadcasted_iota(jnp.int32, (mixed_rows, mixed_rows), 0)
    column = lax.broadcasted_iota(jnp.int32, (mixed_rows, mixed_rows), 1)
    frame = column // step
    frames_within = jnp.where(
        row == (column - frame * step) * seq_count + frame, 1.0, 0.0
    ).astype(BF16)

    def finish(chunk):
        for k in range(1, seq_count):
            out_copy(chunk, k, (seq + seq_count - k) % seq_count).wait_recv()
        for first in range(0, share, step):
            block = jnp.concatenate(
                [arrived[chunk, f, first : first + step, :] for f in range(seq_count)], axis=0
            )
            together[chunk, first * seq_count : first * seq_count + mixed_rows, :] = jnp.dot(
                frames_within, block, preferred_element_type=F32
            ).astype(BF16)
        pltpu.make_async_copy(
            together.at[chunk], result_ref.at[:, out_columns(chunk)], own_sem.at[chunk]
        ).start()

    def work(chunk, carry):
        slab = chunk + 1

        whole_slab(slab)
        project(slab, pl.multiple_of(chunk * CHUNK, CHUNK))

        @pl.when(slab + 2 < slab_count)
        def _():
            pass_x(slab + 2)

        fadings = []
        for block in range(block_count):
            rows = slice(block * GROUP, (block + 1) * GROUP)
            decay = decay_held[chunk, :head_count, rows]
            across = across_held[chunk, :head_count, rows]
            down = down_held[chunk, rows, :head_count]
            closing = down[GROUP - 1 : GROUP, :]
            scale = jnp.exp(closing - down) * (-down_decay_held[chunk, rows, :head_count])
            fading = jnp.exp(closing)
            grown = jnp.exp(down)
            fades = []
            for pair in range(head_count // 2):
                lanes = slice(pair * GROUP, (pair + 1) * GROUP)
                x_pair = mixed[rows, lanes]
                x_wide = x_pair.astype(F32)
                weights = []
                for head in (2 * pair, 2 * pair + 1):
                    gap = down[:, head : head + 1] - across[head : head + 1, :]
                    weights.append(
                        (
                            scores[block]
                            * jnp.exp(jnp.minimum(gap, 0.0))
                            * (-decay[head : head + 1, :])
                        ).astype(BF16)
                    )
                x_apart = jnp.concatenate(
                    [jnp.where(first_head, x_wide, 0.0), jnp.where(first_head, 0.0, x_wide)], axis=0
                ).astype(BF16)
                intra[rows, lanes] = (
                    jnp.dot(
                        jnp.concatenate(weights, axis=1), x_apart, preferred_element_type=F32
                    )
                    + skip_held[chunk, :, lanes] * x_wide
                )
                scaled = (both(scale, pair) * x_wide).astype(BF16)
                block_states[block, :, lanes] = jnp.dot(
                    b_turned[block], scaled, preferred_element_type=F32
                )
                expanded[rows, lanes] = both(grown, pair)
                fades.append(both(fading, pair))
            fadings.append(jnp.concatenate(fades, axis=1))

        @pl.when(slab + 1 < slab_count)
        def _():
            pass_core(slab + 1)

        @pl.when(seq > 0)
        def _():
            state_copy(chunk).wait_recv()

        @pl.when(seq == 0)
        def _():
            arriving_state[chunk] = jnp.zeros(arriving_state.shape[1:], F32)

        state = arriving_state[chunk]
        for block in range(block_count):
            entering_half[block] = state.astype(BF16)
            state = fadings[block] * state + block_states[block]
        leaving_state[chunk] = state

        @pl.when(seq < seq_count - 1)
        def _():
            state_copy(chunk).start()

        gains = out_gain_ref[:, out_columns(chunk)]
        for block in range(block_count):
            rows = slice(block * GROUP, (block + 1) * GROUP)
            inter = jnp.dot(c_held[block], entering_half[block], preferred_element_type=F32)
            ssm = intra[rows, :] + inter * expanded[rows, :]
            square = ssm * ssm
            high = square.astype(BF16)
            low = (square - high.astype(F32)).astype(BF16)
            for pair in range(head_count // 2):
                lanes = slice(pair * GROUP, (pair + 1) * GROUP)
                total = jnp.dot(
                    jnp.concatenate([high[:, lanes], low[:, lanes]], axis=1),
                    same_head_twice,
                    preferred_element_type=F32,
                )
                head_scale = lax.rsqrt(total * (1.0 / head_width) + 1e-05)
                normalized[rows, lanes] = (
                    ssm[:, lanes] * head_scale * gains[:, lanes]
                ).astype(BF16)
        picked[chunk] = jnp.dot(choice[...], normalized[...], preferred_element_type=F32).astype(BF16)
        for k in range(1, seq_count):
            out_copy(chunk, k, seq).start()
        arrived[chunk, seq] = picked[chunk, pl.ds(pl.multiple_of(seq * share, share), share)]

        @pl.when(chunk >= LAG)
        def _():
            finish(chunk - LAG)

        return carry

    lax.fori_loop(0, chunk_count, work, 0)

    for chunk in range(max(chunk_count - LAG, 0), chunk_count):
        finish(chunk)

    def out_settle(chunk, carry):
        for k in range(1, seq_count):
            out_copy(chunk, k, seq).wait_send()
        pltpu.make_async_copy(
            together.at[chunk], result_ref.at[:, out_columns(chunk)], own_sem.at[chunk]
        ).wait()
        return carry

    lax.fori_loop(0, chunk_count, out_settle, 0)

    def settle(slab, carry):
        for k in range(1, z_count):
            z_copy(slab, k, z).wait_send()
        for k in range(1, x_count):
            x_copy(slab, k, x, slice(None)).wait_send()
        if core_count > 1:
            core_copy(slab, core).wait_send()
        return carry

    lax.fori_loop(0, slab_count, settle, 0)

    @pl.when(seq < seq_count - 1)
    def _():
        halo_copy.wait_send()

        def state_settle(chunk, carry):
            state_copy(chunk).wait_send()
            return carry

        lax.fori_loop(0, chunk_count, state_settle, 0)


def on_device(
    sizes, tokens, in_gain, in_weight, conv_weight, conv_bias, log_decay, skip, out_gain, scan_order
):
    z_count, x_count, core_count, seq_count = sizes
    token_count, width = tokens.shape[1:]
    own_rows, channels = in_weight.shape
    heads = log_decay.shape[1]
    inner = out_gain.shape[0]
    head_width = inner // heads
    chunk_count = inner // CHUNK
    slab_count = chunk_count + 1
    per_chunk = heads // chunk_count
    taps = conv_weight.shape[0]
    positions = scan_order.shape[0]
    share = positions // seq_count
    assert token_count == positions and channels == inner + 2 * GROUP and per_chunk == 4

    block_count = token_count // GROUP
    hops = max(z_count - 1, 1), max(x_count - 1, 1), max(seq_count - 1, 1)
    regrouped = pl.pallas_call(
        functools.partial(fused_kernel, sizes + (head_width,)),
        out_shape=jax.ShapeDtypeStruct((token_count, inner), BF16),
        in_specs=[pl.BlockSpec(memory_space=pl.ANY)] * 9,
        out_specs=pl.BlockSpec(memory_space=pl.ANY),
        scratch_shapes=[
            pltpu.VMEM((token_count, width), BF16),
            pltpu.VMEM((1, width), F32),
            pltpu.VMEM((taps, channels), F32),
            pltpu.VMEM((channels,), F32),
            pltpu.VMEM((heads, token_count), F32),
            pltpu.VMEM((1, heads), F32),
            pltpu.VMEM((1, inner), F32),
            pltpu.VMEM((1, positions), jnp.int32),
            pltpu.VMEM((chunk_count, 1, CHUNK), F32),
            pltpu.VMEM((slab_count, 1, CHUNK), F32),
            pltpu.VMEM((chunk_count, seq_count, share, CHUNK), BF16),
            pltpu.VMEM((chunk_count, positions, CHUNK), BF16),
            pltpu.VMEM(
                (slab_count, z_count, x_count, core_count, own_rows // core_count, CHUNK), BF16
            ),
            pltpu.VMEM((HALO + token_count, width), BF16),
            pltpu.VMEM((positions, positions), BF16),
            pltpu.VMEM((chunk_count, token_count, GROUP), F32),
            pltpu.VMEM((chunk_count, token_count, GROUP), F32),
            pltpu.VMEM((chunk_count, 8, token_count), F32),
            pltpu.VMEM((chunk_count, 8, token_count), F32),
            pltpu.VMEM((HALO + token_count, CHUNK), F32),
            pltpu.VMEM((token_count, CHUNK), BF16),
            pltpu.VMEM((token_count // GROUP, GROUP, GROUP), BF16),
            pltpu.VMEM((token_count // GROUP, GROUP, GROUP), BF16),
            pltpu.VMEM((token_count // GROUP, GROUP, GROUP), F32),
            pltpu.VMEM((token_count // GROUP, GROUP, CHUNK), F32),
            pltpu.VMEM((token_count // GROUP, GROUP, CHUNK), BF16),
            pltpu.VMEM((token_count, CHUNK), F32),
            pltpu.VMEM((token_count, CHUNK), F32),
            pltpu.VMEM((chunk_count, GROUP, CHUNK), F32),
            pltpu.VMEM((chunk_count, GROUP, CHUNK), F32),
            pltpu.VMEM((token_count, CHUNK), BF16),
            pltpu.VMEM((chunk_count, positions, CHUNK), BF16),
            pltpu.SemaphoreType.DMA((slab_count, hops[0])),
            pltpu.SemaphoreType.DMA((slab_count, hops[0])),
            pltpu.SemaphoreType.DMA((slab_count, hops[1])),
            pltpu.SemaphoreType.DMA((slab_count, hops[1])),
            pltpu.SemaphoreType.DMA((slab_count,)),
            pltpu.SemaphoreType.DMA((slab_count,)),
            pltpu.SemaphoreType.DMA,
            pltpu.SemaphoreType.DMA,
            pltpu.SemaphoreType.DMA((chunk_count,)),
            pltpu.SemaphoreType.DMA((chunk_count,)),
            pltpu.SemaphoreType.DMA((chunk_count, hops[2])),
            pltpu.SemaphoreType.DMA((chunk_count, hops[2])),
            pltpu.SemaphoreType.DMA((chunk_count,)),
            pltpu.SemaphoreType.DMA((block_count,)),
            pltpu.SemaphoreType.DMA((slab_count,)),
            pltpu.SemaphoreType.DMA((7,)),
        ],
        compiler_params=pltpu.CompilerParams(
            collective_id=0, has_side_effects=True, vmem_limit_bytes=58 * 1024 * 1024
        ),
        name="projected_scan",
    )(
        tokens[0],
        in_gain.reshape(1, width),
        in_weight,
        conv_weight,
        conv_bias,
        log_decay[0],
        skip.reshape(1, heads),
        out_gain.reshape(1, inner),
        scan_order.reshape(1, positions),
    )
    return regrouped[None]


def solution(mesh):
    dp_count, seq_count = mesh.shape["dp"], mesh.shape["seq"]
    x_count = 2 ** (int(math.log2(dp_count)) // 2)
    while dp_count % x_count:
        x_count //= 2
    sizes = (dp_count // x_count, x_count, 2 if seq_count % 2 == 0 else 1, seq_count)
    in_specs = (
        P("dp", "seq", None),
        P(),
        P("dp", None),
        P(),
        P(),
        P("dp", None, "seq"),
        P(),
        P(),
        P(),
    )
    return jax.shard_map(
        functools.partial(on_device, sizes),
        mesh=mesh,
        in_specs=in_specs,
        out_specs=P("dp", "seq", None),
        check_vma=False,
    )
```

profile of v0, /device:TPU:25, one launch (start us, length us, event | category | flops | bytes accessed | tf_op | source)
XLA Modules:
  0.0 93.0 jit_solution(3868152261751797403)
XLA Ops:
  0.0 89.8 %projected_scan.1 = bf16[512,2048]{1,0:T(8,128)(2,1)} custom-call(bf16[512,2048]{1,0:T(8,128)(2,1)} %bitcast.8, f32[1,2048]{1,0:T(1,128)} %bitcast.10, bf16[256,2304]{1,0:T(8,128)(2,1)} %weight_hbm.1, f32[4,2304]{1,0:T(4,128)} %conv_weight_hbm.1, f32[2304]{0:T(1024)} %conv_bias_hbm.1, f32[32,512]{1,0:T(8,128)} %bitcast.9, f32[1,32]{1,0:T(1,128)} %bitcast.13, ...), custom_call_target="tpu_custom_call" | custom-call | tf_op jit(solution)/shard_map/projected_scan/pallas_call | solution.py:528
  89.9 3.2 %copy.11 = bf16[1,512,2048]{2,1,0:T(8,128)(2,1)} copy(bf16[1,512,2048]{2,1,0:T(8,128)(2,1)} %bitcast.7) | data formatting | bytes 4194304
where the time goes:
time: 93.2 us; the launch traced here: 93 us
  Pallas kernels  89.8 us (96%)
  local copies, waits for them, and re-layouts  3.16 us (3%)
    pallas_call x1, Pallas kernels, on_device(): pl.pallas_call(functools.partial(fused_kernel, sizes + (head_width,)), ou...  89.8 us
    unnamed x1, local copies, waits for them, and re-layouts  3.16 us

commit v1 on v0

--- a/solution.py
+++ b/solution.py
@@ -12,6 +12,7 @@
 CHUNK = 256
 HALO = 16
 WINDOW = 3
+SPLIT = 3
 LAG = 2
 BF16 = jnp.bfloat16
 F32 = jnp.float32
@@ -66,6 +67,8 @@
     z_recv,
     x_send,
     x_recv,
+    y_send,
+    y_recv,
     core_send,
     core_recv,
     halo_send,
@@ -86,8 +89,10 @@
     z = dp // x_count
     x = dp % x_count
     core = seq % core_count
+    planes = slabs.shape[2]
+    plane = seq // core_count % planes
     sibling = seq - core + (core + 1) % core_count
-    half = slabs.shape[4]
+    half = slabs.shape[5]
     slab_count = slabs.shape[0]
     chunk_count = slab_count - 1
     token_count, width = tokens_ref.shape
@@ -102,13 +107,34 @@
     for partner in partners:
         pl.semaphore_signal(barrier, inc=1, device_id=partner, device_id_type=MESH)
 
+    def is_split(slab):
+        if planes == 1:
+            return False
+        if isinstance(slab, int):
+            return slab > 0 and slab % SPLIT == 0
+        return jnp.logical_and(slab > 0, slab % SPLIT == 0)
+
+    def where_true(condition, act):
+        if isinstance(condition, bool):
+            if condition:
+                act()
+        else:
+            pl.when(condition)(act)
+
+    def where_carried(slab, row, act):
+        split = is_split(slab)
+        if split is False:
+            act()
+        else:
+            pl.when(jnp.logical_or(jnp.logical_not(split), row % planes == plane))(act)
+
     own_rows = pl.ds(pl.multiple_of(core * half, half), half)
 
     def load_weight(slab):
         first = chunk_count * CHUNK if slab == 0 else (slab - 1) * CHUNK
         return pltpu.make_async_copy(
             weight_hbm.at[own_rows, first : first + CHUNK],
-            slabs.at[slab, z, x, core],
+            slabs.at[slab, z // planes, z % planes, x, core],
             weight_sem.at[slab],
         )
 
@@ -131,19 +157,19 @@
         )
     ]
     for slab in range(slab_count):
-        load_weight(slab).start()
+        where_carried(slab, z, load_weight(slab).start)
     for block in range(block_count):
         load_tokens(block).start()
     for copy in small:
         copy.start()
     for slab in range(slab_count):
-        load_weight(slab).wait()
+        where_carried(slab, z, load_weight(slab).wait)
     pl.semaphore_wait(barrier, len(partners))
 
     def z_copy(slab, k, source):
         return pltpu.make_async_remote_copy(
-            src_ref=slabs.at[slab, source, x, core],
-            dst_ref=slabs.at[slab, source, x, core],
+            src_ref=slabs.at[slab, source // planes, source % planes, x, core],
+            dst_ref=slabs.at[slab, source // planes, source % planes, x, core],
             send_sem=z_send.at[slab, k - 1],
             recv_sem=z_recv.at[slab, k - 1],
             device_id=(((z + k) % z_count) * x_count + x, seq),
@@ -151,7 +177,12 @@
         )
 
     def x_copy(slab, k, source, row):
-        piece = slabs.at[slab, row, source, core]
+        if row is None:
+            piece = slabs.at[slab, :, :, source, core]
+        elif isinstance(row, str):
+            piece = slabs.at[slab, :, plane, source, core]
+        else:
+            piece = slabs.at[slab, row // planes, row % planes, source, core]
         return pltpu.make_async_remote_copy(
             src_ref=piece,
             dst_ref=piece,
@@ -163,26 +194,49 @@
 
     def core_copy(slab, source):
         return pltpu.make_async_remote_copy(
-            src_ref=slabs.at[slab, :, :, source],
-            dst_ref=slabs.at[slab, :, :, source],
+            src_ref=slabs.at[slab, :, :, :, source],
+            dst_ref=slabs.at[slab, :, :, :, source],
             send_sem=core_send.at[slab],
             recv_sem=core_recv.at[slab],
             device_id=(dp, sibling),
             device_id_type=MESH,
         )
 
+    def y_copy(slab, k, source):
+        piece = slabs.at[slab, :, source, :, core]
+        return pltpu.make_async_remote_copy(
+            src_ref=piece,
+            dst_ref=piece,
+            send_sem=y_send.at[slab // SPLIT - 1, k - 1],
+            recv_sem=y_recv.at[slab // SPLIT - 1, k - 1],
+            device_id=(dp, (plane + k) % planes * core_count + core),
+            device_id_type=MESH,
+        )
+
+    def where_split(slab, act, otherwise):
+        split = is_split(slab)
+        where_true(split, act)
+        where_true(not split if isinstance(split, bool) else jnp.logical_not(split), otherwise)
+
     def send_own(slab):
-        for k in range(1, z_count):
-            z_copy(slab, k, z).start()
-        for k in range(1, x_count):
-            x_copy(slab, k, x, z).start()
+        def act():
+            for k in range(1, z_count):
+                z_copy(slab, k, z).start()
+            for k in range(1, x_count):
+                x_copy(slab, k, x, z).start()
+
+        where_carried(slab, z, act)
 
     def pass_x(slab):
         for k in range(1, z_count):
             row = (z + z_count - k) % z_count
-            z_copy(slab, k, row).wait_recv()
-            for kx in range(1, x_count):
-                x_copy(slab, kx, x, row).start()
+
+            def act(k=k, row=row):
+                z_copy(slab, k, row).wait_recv()
+                for kx in range(1, x_count):
+                    x_copy(slab, kx, x, row).start()
+
+            where_carried(slab, row, act)
 
         if isinstance(slab, int):
             if slab + WINDOW < slab_count:
@@ -193,9 +247,24 @@
             def _():
                 send_own(slab + WINDOW)
 
+    def x_arrived(slab, rows):
+        for k in range(1, x_count):
+            x_copy(slab, k, (x + x_count - k) % x_count, rows).wait_recv()
+
+    def pass_y(slab):
+        def act():
+            x_arrived(slab, "plane")
+            for k in range(1, planes):
+                y_copy(slab, k, plane).start()
+
+        where_true(is_split(slab), act)
+
     def pass_core(slab):
-        for k in range(1, x_count):
-            x_copy(slab, k, (x + x_count - k) % x_count, slice(None)).wait_recv()
+        def y_arrived():
+            for k in range(1, planes):
+                y_copy(slab, k, (plane + planes - k) % planes).wait_recv()
+
+        where_split(slab, y_arrived, lambda: x_arrived(slab, None))
         if core_count > 1:
             core_copy(slab, core).start()
 
@@ -421,6 +490,10 @@
         def _():
             pass_core(slab + 1)
 
+        @pl.when(slab + 2 < slab_count)
+        def _():
+            pass_y(slab + 2)
+
         @pl.when(seq > 0)
         def _():
             state_copy(chunk).wait_recv()
@@ -486,9 +559,17 @@
 
     def settle(slab, carry):
         for k in range(1, z_count):
-            z_copy(slab, k, z).wait_send()
+            where_carried(slab, z, z_copy(slab, k, z).wait_send)
         for k in range(1, x_count):
-            x_copy(slab, k, x, slice(None)).wait_send()
+            where_split(
+                slab, x_copy(slab, k, x, "plane").wait_send, x_copy(slab, k, x, None).wait_send
+            )
+
+        def y_settle():
+            for k in range(1, planes):
+                y_copy(slab, k, plane).wait_send()
+
+        where_true(is_split(slab), y_settle)
         if core_count > 1:
             core_copy(slab, core).wait_send()
         return carry
@@ -524,6 +605,9 @@
     assert token_count == positions and channels == inner + 2 * GROUP and per_chunk == 4
 
     block_count = token_count // GROUP
+    planes = seq_count // core_count
+    if z_count % planes:
+        planes = 1
     hops = max(z_count - 1, 1), max(x_count - 1, 1), max(seq_count - 1, 1)
     regrouped = pl.pallas_call(
         functools.partial(fused_kernel, sizes + (head_width,)),
@@ -544,7 +628,16 @@
             pltpu.VMEM((chunk_count, seq_count, share, CHUNK), BF16),
             pltpu.VMEM((chunk_count, positions, CHUNK), BF16),
             pltpu.VMEM(
-                (slab_count, z_count, x_count, core_count, own_rows // core_count, CHUNK), BF16
+                (
+                    slab_count,
+                    z_count // planes,
+                    planes,
+                    x_count,
+                    core_count,
+                    own_rows // core_count,
+                    CHUNK,
+                ),
+                BF16,
             ),
             pltpu.VMEM((HALO + token_count, width), BF16),
             pltpu.VMEM((positions, positions), BF16),
@@ -569,6 +662,8 @@
             pltpu.SemaphoreType.DMA((slab_count, hops[0])),
             pltpu.SemaphoreType.DMA((slab_count, hops[1])),
             pltpu.SemaphoreType.DMA((slab_count, hops[1])),
+            pltpu.SemaphoreType.DMA((slab_count // SPLIT, max(planes - 1, 1))),
+            pltpu.SemaphoreType.DMA((slab_count // SPLIT, max(planes - 1, 1))),
             pltpu.SemaphoreType.DMA((slab_count,)),
             pltpu.SemaphoreType.DMA((slab_count,)),
             pltpu.SemaphoreType.DMA,

time: 93.2 us -> 107 us (1.15)
  Pallas kernels: 89.8 us -> 103 us
    pallas_call x1, Pallas kernels: 89.8 us -> 103 us  [on_device(): pl.pallas_call(functools.partial(fused_kernel, sizes + (head_width,)), ou...]
where the time goes in v1:
time: 107 us; the launch traced here: 106 us
  Pallas kernels  103 us (96%)
  local copies, waits for them, and re-layouts  3.16 us (3%)
    pallas_call x1, Pallas kernels, on_device(): pl.pallas_call(functools.partial(fused_kernel, sizes + (head_width,)), ou...  103 us
    unnamed x1, local copies, waits for them, and re-layouts  3.16 us

profile of v1, /device:TPU:25, one launch (start us, length us, event | category | flops | bytes accessed | tf_op | source)
XLA Modules:
  0.0 106.3 jit_solution(14057731886787538030)
XLA Ops:
  0.0 103.1 %projected_scan.1 = bf16[512,2048]{1,0:T(8,128)(2,1)} custom-call(bf16[512,2048]{1,0:T(8,128)(2,1)} %bitcast.8, f32[1,2048]{1,0:T(1,128)} %bitcast.10, bf16[256,2304]{1,0:T(8,128)(2,1)} %weight_hbm.1, f32[4,2304]{1,0:T(4,128)} %conv_weight_hbm.1, f32[2304]{0:T(1024)} %conv_bias_hbm.1, f32[32,512]{1,0:T(8,128)} %bitcast.9, f32[1,32]{1,0:T(1,128)} %bitcast.13, ...), custom_call_target="tpu_custom_call" | custom-call | tf_op jit(solution)/shard_map/projected_scan/pallas_call | solution.py:612
  103.1 3.2 %copy.11 = bf16[1,512,2048]{2,1,0:T(8,128)(2,1)} copy(bf16[1,512,2048]{2,1,0:T(8,128)(2,1)} %bitcast.7) | data formatting | bytes 4194304

commit v2 on v1

--- a/solution.py
+++ b/solution.py
@@ -12,7 +12,7 @@
 CHUNK = 256
 HALO = 16
 WINDOW = 3
-SPLIT = 3
+SPLIT = 2
 LAG = 2
 BF16 = jnp.bfloat16
 F32 = jnp.float32
@@ -111,8 +111,8 @@
         if planes == 1:
             return False
         if isinstance(slab, int):
-            return slab > 0 and slab % SPLIT == 0
-        return jnp.logical_and(slab > 0, slab % SPLIT == 0)
+            return 0 < slab <= SPLIT
+        return jnp.logical_and(slab > 0, slab <= SPLIT)
 
     def where_true(condition, act):
         if isinstance(condition, bool):
@@ -207,8 +207,8 @@
         return pltpu.make_async_remote_copy(
             src_ref=piece,
             dst_ref=piece,
-            send_sem=y_send.at[slab // SPLIT - 1, k - 1],
-            recv_sem=y_recv.at[slab // SPLIT - 1, k - 1],
+            send_sem=y_send.at[slab - 1, k - 1],
+            recv_sem=y_recv.at[slab - 1, k - 1],
             device_id=(dp, (plane + k) % planes * core_count + core),
             device_id_type=MESH,
         )
@@ -364,6 +364,7 @@
             decay_held[chunk, :head_count, rows] = decay[heads, :]
     pass_core(0)
     pass_x(1)
+    pass_y(1)
     choice[...] = jnp.transpose(
         jnp.where(
             lax.broadcasted_iota(jnp.int32, (positions, positions), 0) == order_ref[...], 1.0, 0.0
@@ -377,7 +378,7 @@
     whole_slab(0)
     project(0, chunk_count * CHUNK)
     pass_x(2)
-    pass_core(1)
+    pass_y(2)
     for block in range(block_count):
         rows = slice(block * GROUP, (block + 1) * GROUP)
         b_block = mixed[rows, :GROUP]
@@ -387,6 +388,8 @@
         scores[block] = jnp.where(
             causal, jnp.dot(c_block, b_turned[block], preferred_element_type=F32), 0.0
         )
+    pass_core(1)
+
     def state_copy(chunk):
         return pltpu.make_async_remote_copy(
             src_ref=leaving_state.at[chunk],
@@ -490,23 +493,19 @@
         def _():
             pass_core(slab + 1)
 
-        @pl.when(slab + 2 < slab_count)
-        def _():
-            pass_y(slab + 2)
-
         @pl.when(seq > 0)
         def _():
             state_copy(chunk).wait_recv()
 
         @pl.when(seq == 0)
         def _():
-            arriving_state[chunk] = jnp.zeros(arriving_state.shape[1:], F32)
-
-        state = arriving_state[chunk]
+            arriving_state[chunk] = jnp.zeros(arriving_state.shape[1:], BF16)
+
+        state = arriving_state[chunk].astype(F32)
         for block in range(block_count):
             entering_half[block] = state.astype(BF16)
             state = fadings[block] * state + block_states[block]
-        leaving_state[chunk] = state
+        leaving_state[chunk] = state.astype(BF16)
 
         @pl.when(seq < seq_count - 1)
         def _():
@@ -654,16 +653,16 @@
             pltpu.VMEM((token_count // GROUP, GROUP, CHUNK), BF16),
             pltpu.VMEM((token_count, CHUNK), F32),
             pltpu.VMEM((token_count, CHUNK), F32),
-            pltpu.VMEM((chunk_count, GROUP, CHUNK), F32),
-            pltpu.VMEM((chunk_count, GROUP, CHUNK), F32),
+            pltpu.VMEM((chunk_count, GROUP, CHUNK), BF16),
+            pltpu.VMEM((chunk_count, GROUP, CHUNK), BF16),
             pltpu.VMEM((token_count, CHUNK), BF16),
             pltpu.VMEM((chunk_count, positions, CHUNK), BF16),
             pltpu.SemaphoreType.DMA((slab_count, hops[0])),
             pltpu.SemaphoreType.DMA((slab_count, hops[0])),
             pltpu.SemaphoreType.DMA((slab_count, hops[1])),
             pltpu.SemaphoreType.DMA((slab_count, hops[1])),
-            pltpu.SemaphoreType.DMA((slab_count // SPLIT, max(planes - 1, 1))),
-            pltpu.SemaphoreType.DMA((slab_count // SPLIT, max(planes - 1, 1))),
+            pltpu.SemaphoreType.DMA((SPLIT, max(planes - 1, 1))),
+            pltpu.SemaphoreType.DMA((SPLIT, max(planes - 1, 1))),
             pltpu.SemaphoreType.DMA((slab_count,)),
             pltpu.SemaphoreType.DMA((slab_count,)),
             pltpu.SemaphoreType.DMA,

time: 107 us -> 86.6 us (0.81)
  Pallas kernels: 103 us -> 83.2 us
    pallas_call x1, Pallas kernels: 103 us -> 83.2 us  [on_device(): pl.pallas_call(functools.partial(fused_kernel, sizes + (head_width,)), ou...]
where the time goes in v2:
time: 86.6 us; the launch traced here: 86.3 us
  Pallas kernels  83.2 us (96%)
  local copies, waits for them, and re-layouts  3.16 us (4%)
    pallas_call x1, Pallas kernels, on_device(): pl.pallas_call(functools.partial(fused_kernel, sizes + (head_width,)), ou...  83.2 us
    unnamed x1, local copies, waits for them, and re-layouts  3.16 us

profile of v2, /device:TPU:25, one launch (start us, length us, event | category | flops | bytes accessed | tf_op | source)
XLA Modules:
  0.0 86.3 jit_solution(1994226095639003934)
XLA Ops:
  0.0 83.2 %projected_scan.1 = bf16[512,2048]{1,0:T(8,128)(2,1)} custom-call(bf16[512,2048]{1,0:T(8,128)(2,1)} %bitcast.8, f32[1,2048]{1,0:T(1,128)} %bitcast.10, bf16[256,2304]{1,0:T(8,128)(2,1)} %weight_hbm.1, f32[4,2304]{1,0:T(4,128)} %conv_weight_hbm.1, f32[2304]{0:T(1024)} %conv_bias_hbm.1, f32[32,512]{1,0:T(8,128)} %bitcast.9, f32[1,32]{1,0:T(1,128)} %bitcast.13, ...), custom_call_target="tpu_custom_call" | custom-call | tf_op jit(solution)/shard_map/projected_scan/pallas_call | solution.py:611
  83.2 3.2 %copy.11 = bf16[1,512,2048]{2,1,0:T(8,128)(2,1)} copy(bf16[1,512,2048]{2,1,0:T(8,128)(2,1)} %bitcast.7) | data formatting | bytes 4194304
